TPU v7x, 512 devices: a whole 4x4x16 slice. The times are simulated.
512 devices in a mesh: aux: 64 (over y, z), occ: 8 (over x, core).
Axes of the slice: x: 4, y: 4, z: 16, core: 2. Of those that a mesh axis runs over, the one named last changes fastest.
Arguments:
- factor_tiles: bfloat16 [128, 24, 4, 128, 128], P('aux'), may hold values from -1 to 1
- tile_cols: int32 [128, 24, 4], P('aux'), may hold values from 0 to 23, as said below
- coeffs: bfloat16 [3072, 256], P(None, 'occ'), may hold values from -0.25 to 0.25
- pair_owner: int32 [576], P('aux'), may hold values from 0 to 575, each once
Outputs:
- exchange_tiles: float32 [576, 128, 128], P('aux', 'occ')
Inputs may be any that keep to these rules, and one draw needn't show every extreme that they name: `tile_cols`: for each auxiliary function and basis block row, the 4 listed column blocks are distinct. `pair_owner`: each basis block pair appears exactly once.
All inputs are finite; a program needn't handle non-finite values.
Results may differ from a plain program's by a relative error of at most 0.0015.
Values may be sent and summed in bfloat16 or wider, within the bound.
A program may use at most 128 MiB of HBM per device.

v0:
```python
import jax
import jax.numpy as jnp
from jax import lax
from jax.sharding import PartitionSpec as P


def shards(factor_tiles, tile_cols, coeffs, pair_owner):
    aux_count = factor_tiles.shape[0]
    block_count = factor_tiles.shape[1]
    tile_width = factor_tiles.shape[3]
    local_occ = coeffs.shape[1]
    blocks = coeffs.reshape(block_count, tile_width, local_occ)
    picked = blocks[tile_cols]
    halves = jnp.einsum(
        "qmsrl,qmsli->mrqi", factor_tiles, picked, preferred_element_type=jnp.float32
    ).astype(jnp.bfloat16)
    halves = halves.reshape(block_count, tile_width, aux_count * local_occ)
    row_blocks = pair_owner // block_count
    col_blocks = pair_owner % block_count
    gathered = lax.all_gather(halves, "aux", axis=2, tiled=True)
    row_part = jnp.take(gathered, row_blocks, axis=0)
    col_part = jnp.take(gathered, col_blocks, axis=0)
    partial_tiles = jnp.einsum(
        "sbw,scw->sbc", row_part, col_part, preferred_element_type=jnp.float32
    )
    summed = lax.psum(partial_tiles, "occ")
    share_rows = tile_width // lax.axis_size("occ")
    return lax.dynamic_slice_in_dim(summed, lax.axis_index("occ") * share_rows, share_rows, 1)


def solution(mesh):
    placed = (P("aux", None, None, None, None), P("aux", None, None), P(None, "occ"), P("aux"))
    return jax.shard_map(
        shards, mesh=mesh, in_specs=placed, out_specs=P("aux", "occ", None), check_vma=False
    )
```

profile of v0, /device:TPU:1, one launch (start us, length us, event | category | flops | bytes accessed | tf_op | source)
XLA Modules:
  0.0 413.2 jit_solution(6229224219525203429)
XLA Ops:
  6.5 0.0 copy-start
  6.5 0.0 all-gather.2.cloned.1.call-start
  6.5 0.9 copy-done
  7.5 0.7 compare_select_fusion
  8.2 0.1 copy.15
  8.3 0.1 reshape.31
  8.4 0.0 copy-start.2
  8.4 0.9 gather_fusion
  9.3 5.0 %fusion.14 = bf16[24,2,32,128]{3,2,1,0:T(8,128)(2,1)S(1)} fusion(bf16[2,24,4,128,128]{4,3,2,1,0:T(8,128)(2,1)} %param.6, bf16[2,24,4,128,32]{3,4,2,1,0:T(8,128)(2,1)S(1)} %bitcast.14), kind=kOutput, calls=%fused_computation.13 | convolution fusion | flops 201523200 | bytes 8257536 | tf_op jit(solution)/shard_map/qmsrl,qmsli->mrqi/dot_general | solution.py:14
  14.3 1.0 copy.19
  15.3 0.0 all-gather.2.cloned.1.call-update
  15.3 0.0 all-reduce.2.cloned.1.call-start
  15.4 0.0 copy-done.2
  15.4 249.4 %all-gather.2.cloned.1.call-done = bf16[24,128,4096]{1,0,2:T(8,128)(2,1)} async-done(((bf16[24,128,64]{1,0,2:T(8,128)(2,1)}), bf16[24,128,4096]{1,0,2:T(8,128)(2,1)}) %all-gather.2.cloned.1.call-update) | async-done | bytes 25165840 | tf_op jit(solution)/shard_map/all_gather | solution.py:20
  264.8 31.6 %copy.20 = bf16[24,128,4096]{2,1,0:T(8,128)(2,1)} copy(bf16[24,128,4096]{1,0,2:T(8,128)(2,1)} %all-gather.2.cloned.1.call-done) | data formatting | bytes 50331648 | tf_op jit(solution)/shard_map/all_gather | solution.py:20
  296.4 13.1 %gather_fusion.2 = bf16[9,128,4096]{2,1,0:T(8,128)(2,1)} fusion(bf16[24,128,4096]{2,1,0:T(8,128)(2,1)} %copy.20, s32[1024]{0:T(1024)S(1)} %get-tuple-element.12), kind=kCustom, calls=%fused_computation.1.clone | custom fusion | bytes 18874404 | tf_op jit(solution)/shard_map/jit(_take)/gather | solution.py:22
  309.5 13.3 %gather_fusion.1 = bf16[9,128,4096]{2,1,0:T(8,128)(2,1)} fusion(bf16[24,128,4096]{2,1,0:T(8,128)(2,1)} %copy.20, s32[1024]{0:T(1024)S(1)} %get-tuple-element.13), kind=kCustom, calls=%fused_computation.clone | custom fusion | bytes 18874404 | tf_op jit(solution)/shard_map/jit(_take)/gather | solution.py:21
  322.8 0.0 copy-start.1
  322.8 10.0 %fusion = f32[9,128,128]{2,1,0:T(8,128)} fusion(bf16[9,128,4096]{2,1,0:T(8,128)(2,1)} %gather_fusion.2, bf16[9,128,4096]{2,1,0:T(8,128)(2,1)} %gather_fusion.1, pred[9]{0:T(512)(128)(4,1)S(1)} %get-tuple-element.10, pred[9]{0:T(512)(128)(4,1)S(1)} %get-tuple-element.6), kind=kOutput, calls=%fused_computation.3 | convolution fusion | flops 1217396736 | bytes 19464210 | tf_op jit(solution)/shard_map/sbw,scw->sbc/dot_general | solution.py:23
  332.8 0.0 all-reduce.2.cloned.1.call-update
  332.8 72.0 %all-reduce.2.cloned.1.call-done = f32[9,128,128]{2,1,0:T(8,128)} async-done(((f32[9,128,128]{2,1,0:T(8,128)}), f32[9,128,128]{2,1,0:T(8,128)}) %all-reduce.2.cloned.1.call-update) | async-done | bytes 589840 | tf_op jit(solution)/shard_map/psum | solution.py:26
  404.8 1.5 constant_dynamic-slice_fusion
  406.3 0.0 copy-done.1
  (4 shorter events, 0.1 us)
Async XLA Ops:
  6.5 0.9 copy-start
  6.5 258.2 %all-gather.2.cloned.1.call-start = ((), (), s32[]{:S(2)}) async-start(), calls=%async_computation | async-start | bytes 25559040 | tf_op jit(solution)/shard_map/all_gather | solution.py:20
  8.4 7.0 %copy-start.2 = (s32[9]{0:T(128)S(1)}, s32[9]{0:T(128)}, u32[]{:S(2)}) copy-start(s32[9]{0:T(128)} %param.9) | copy-start | bytes 112
  15.3 389.5 %all-reduce.2.cloned.1.call-start = ((), (), s32[]{:S(2)}) async-start(), calls=%async_computation.1 | async-start | bytes 1179648 | tf_op jit(solution)/shard_map/psum | solution.py:26
  322.8 83.5 %copy-start.1 = (bf16[3072,32]{0,1:T(8,128)(2,1)S(1)}, bf16[3072,32]{0,1:T(8,128)(2,1)}, u32[]{:S(2)}) copy-start(bf16[3072,32]{0,1:T(8,128)(2,1)} %param.8) | copy-start | bytes 589828
Sparse Core Ops, SparseCore 0:
  15.4 249.3 all-gather.1
  333.0 71.8 all-reduce.1
where the time goes:
time: 415 us; the launch traced here: 413 us
  waiting for transfers between devices  321 us (77%)
  local copies, waits for them, and re-layouts  62.6 us (15%)
  matrix products  15 us (4%)
  between operations  13.5 us (3%)
    all_gather x1, waiting for transfers between devices, shards(): gathered = lax.all_gather(halves, 'aux', axis=2, tiled=True)  249 us
    psum x1, waiting for transfers between devices, shards(): summed = lax.psum(partial_tiles, 'occ')  72 us
    all_gather x1, local copies, waits for them, and re-layouts, shards(): gathered = lax.all_gather(halves, 'aux', axis=2, tiled=True)  31.6 us
    gather x1, local copies, waits for them, and re-layouts, shards(): row_part = jnp.take(gathered, row_blocks, axis=0)  13.3 us
    gather x1, local copies, waits for them, and re-layouts, shards(): col_part = jnp.take(gathered, col_blocks, axis=0)  13.1 us
    dot_general x1, matrix products, shards(): jnp.einsum('sbw,scw->sbc', row_part, col_part, preferred_element_type=jnp...  10 us
  transfers between devices with their start and end apart: 2, of which 2 were waited for; matrix products, arithmetic and copies ran while one was open for 0% of the time, Pallas kernels for 0%

commit v1 on v0

v1 whole, which is shorter than its diff:
```python
import jax
import jax.numpy as jnp
from jax import lax
from jax.experimental import pallas as pl
from jax.experimental.pallas import tpu as pltpu
from jax.sharding import PartitionSpec as P

NT = (((1,), (1,)), ((), ()))


def partial_kernel(cols, owners, share, factor, coeffs_t, out, half, mine, tiles):
    m = pl.program_id(0)
    aux_count, _, entries, blk, _ = factor.shape
    occ = coeffs_t.shape[0]
    nb = cols.shape[0] // (aux_count * entries)
    rows = out.shape[1]
    for q in range(aux_count):
        left, right = [], []
        for s in range(entries):
            col = cols[(q * nb + m) * entries + s]
            left.append(factor[q, 0, s])
            right.append(coeffs_t[:, pl.ds(pl.multiple_of(col * blk, blk), blk)])
        done = lax.dot_general(
            jnp.concatenate(left, axis=1),
            jnp.concatenate(right, axis=1),
            NT,
            preferred_element_type=jnp.float32,
        )
        half[pl.ds(pl.multiple_of(m * blk, blk), blk), q * occ : (q + 1) * occ] = done.astype(
            jnp.bfloat16
        )
    first = pl.multiple_of(m * blk + share[0] * rows, rows)
    mine[pl.ds(pl.multiple_of(m * rows, rows), rows), :] = half[pl.ds(first, rows), :]

    @pl.when(m == nb - 1)
    def _():
        def pair(p, carry):
            part = half[pl.ds(pl.multiple_of(p * 2 * blk, 2 * blk), 2 * blk), :]
            prod = lax.dot_general(mine[...], part, NT, preferred_element_type=jnp.float32)
            tiles[2 * p] = prod[:, :blk]
            tiles[2 * p + 1] = prod[:, blk:]
            return carry

        lax.fori_loop(0, nb // 2, pair, 0)

        def pick(k, carry):
            pair_index = owners[k]
            a, b = pair_index // nb, pair_index % nb
            out[k] = tiles[b, pl.ds(pl.multiple_of(a * rows, rows), rows), :]
            return carry

        lax.fori_loop(0, nb * nb, pick, 0)


def shards(factor_tiles, tile_cols, coeffs, pair_owner):
    aux_count, nb, entries, blk, _ = factor_tiles.shape
    occ_ways = lax.axis_size("occ")
    rows = blk // occ_ways
    occ = coeffs.shape[1] * occ_ways
    coeffs_t = lax.all_gather(coeffs.T, "occ", axis=0, tiled=True)
    owners = lax.all_gather(pair_owner, "aux", axis=0, tiled=True)
    share = lax.axis_index("occ").astype(jnp.int32).reshape(1)
    partial = pl.pallas_call(
        partial_kernel,
        grid_spec=pltpu.PrefetchScalarGridSpec(
            num_scalar_prefetch=3,
            grid=(nb,),
            in_specs=[
                pl.BlockSpec((aux_count, 1, entries, blk, blk), lambda m, *_: (0, m, 0, 0, 0)),
                pl.BlockSpec((occ, nb * blk), lambda m, *_: (0, 0)),
            ],
            out_specs=pl.BlockSpec((nb * nb, rows, blk), lambda m, *_: (0, 0, 0)),
            scratch_shapes=[
                pltpu.VMEM((nb * blk, aux_count * occ), jnp.bfloat16),
                pltpu.VMEM((nb * rows, aux_count * occ), jnp.bfloat16),
                pltpu.VMEM((nb, nb * rows, blk), jnp.float32),
            ],
        ),
        out_shape=jax.ShapeDtypeStruct((nb * nb, rows, blk), jnp.float32),
        compiler_params=pltpu.CompilerParams(vmem_limit_bytes=48 * 2**20),
    )(tile_cols.reshape(-1), owners, share, factor_tiles, coeffs_t)
    return lax.psum_scatter(partial, "aux", scatter_dimension=0, tiled=True)


def solution(mesh):
    placed = (P("aux", None, None, None, None), P("aux", None, None), P(None, "occ"), P("aux"))
    return jax.shard_map(
        shards, mesh=mesh, in_specs=placed, out_specs=P("aux", "occ", None), check_vma=False
    )
```

time: 415 us -> 792 us (1.91); the launches traced: 413 us -> 782 us
  waiting for transfers between devices: 321 us -> 701 us
  local copies, waits for them, and re-layouts: 62.6 us -> 4.41 us
  Pallas kernels: 0 us -> 32.1 us
  blocking collectives: 0 us -> 30.2 us
  matrix products: 15 us -> 0 us
    reduce_scatter x0 -> x1, waiting for transfers between devices: none -> 694 us  [shards(): return lax.psum_scatter(partial, 'aux', scatter_dimension=0, tiled=True)]
    all_gather x1, waiting for transfers between devices: 249 us -> 6.04 us  [shards(): coeffs_t = lax.all_gather(coeffs.T, 'occ', axis=0, tiled=True)]
    psum x1 -> x0, waiting for transfers between devices: 72 us -> none  [shards(): summed = lax.psum(partial_tiles, 'occ')]
    pallas_call x0 -> x1, Pallas kernels: none -> 32.1 us  [shards(): pl.pallas_call(partial_kernel, grid_spec=pltpu.PrefetchScalarGridSpec(num...]
    all_gather x1 -> x0, local copies, waits for them, and re-layouts: 31.6 us -> none  [shards(): gathered = lax.all_gather(halves, 'aux', axis=2, tiled=True)]
    unnamed x0 -> x1, blocking collectives: none -> 30.2 us
    gather x3 -> x0, local copies, waits for them, and re-layouts: 27.3 us -> none  [the longest x1 13.3 us: shards(): row_part = jnp.take(gathered, row_blocks, axis=0)]
    dot_general x2 -> x0, matrix products: 15 us -> none  [the longest x1 10 us: shards(): jnp.einsum('sbw,scw->sbc', row_part, col_part, preferred_element_type=jnp...]
where the time goes in v1:
time: 792 us; the launch traced here: 782 us
  waiting for transfers between devices  701 us (89%)
  Pallas kernels  32.1 us (4%)
  blocking collectives  30.2 us (4%)
  between operations  14.1 us (2%)
    reduce_scatter x1, waiting for transfers between devices, shards(): return lax.psum_scatter(partial, 'aux', scatter_dimension=0, tiled=True)  694 us
    pallas_call x1, Pallas kernels, shards(): pl.pallas_call(partial_kernel, grid_spec=pltpu.PrefetchScalarGridSpec(num...  32.1 us
    unnamed x1, blocking collectives  30.2 us
  transfers between devices with their start and end apart: 2, of which 2 were waited for; matrix products, arithmetic and copies ran while one was open for 0% of the time, Pallas kernels for 0%

profile of v1, /device:TPU:1, one launch (start us, length us, event | category | flops | bytes accessed | tf_op | source)
XLA Modules:
  0.0 781.6 jit_solution(13295679787491565950)
XLA Ops:
  6.5 0.0 all-gather.2.cloned.1.call-start
  6.5 0.7 all-gather.2.cloned.1.call-update
  7.3 0.0 reduce-scatter.2.cloned.1.call-start
  7.3 0.8 copy.5
  8.1 0.1 reshape.6.cols
  8.2 1.3 dynamic-slice
  10.1 0.9 dynamic-update-slice
  11.0 30.2 %all-reduce.owners = s32[576]{0:T(1024)S(1)} all-reduce(s32[576]{0:T(1024)S(1)} %dynamic-update-slice), channel_id=1, replica_groups=mesh['aux'=64,'occ'=8] {'aux'}, use_global_device_ids=true, to_apply=%add | all-reduce | flops 576 | bytes 4608
  41.2 6.0 all-gather.2.cloned.1.call-done.coeffs_t
  47.2 0.0 copy-start
  47.2 1.4 copy-done
  48.6 32.1 %shard_map.46 = f32[576,16,128]{2,1,0:T(8,128)} custom-call(s32[192]{0:T(256)S(1)} %reshape.6.cols, s32[576]{0:T(1024)S(1)} %all-reduce.owners, s32[1]{0:T(128)} %bitcast.1.share, bf16[2,24,4,128,128]{4,3,2,1,0:T(8,128)(2,1)} %factor.1, bf16[256,3072]{1,0:T(8,128)(2,1)S(1)} %copy-done), custom_call_target="tpu_custom_call" | custom-call | tf_op jit(solution)/shard_map/pallas_call | solution.py:63
  80.7 0.0 reduce-scatter.2.cloned.1.call-update
  80.7 694.0 %reduce-scatter.2.cloned.1.call-done = f32[9,16,128]{2,1,0:T(8,128)} async-done(((f32[576,16,128]{2,1,0:T(8,128)}), f32[9,16,128]{2,1,0:T(8,128)}) %reduce-scatter.2.cloned.1.call-update) | async-done | bytes 73744 | tf_op jit(solution)/shard_map/reduce_scatter | solution.py:82
  (1 shorter events, 0.0 us)
Async XLA Ops:
  6.5 40.7 %all-gather.2.cloned.1.call-start = ((), (), s32[]{:S(2)}) async-start(), calls=%async_computation.1 | async-start | bytes 1769472 | tf_op jit(solution)/shard_map/all_gather | solution.py:60
  7.3 767.5 %reduce-scatter.2.cloned.1.call-start = ((), (), s32[]{:S(2)}) async-start(), calls=%async_computation.2 | async-start | bytes 4792320 | tf_op jit(solution)/shard_map/reduce_scatter | solution.py:82
  47.2 1.4 copy-start
Sparse Core Ops, SparseCore 0:
  9.5 37.6 all-gather.1
  80.8 693.8 reduce-scatter.1

commit v2 on v1

--- a/solution.py
+++ b/solution.py
@@ -6,14 +6,18 @@
 from jax.sharding import PartitionSpec as P
 
 NT = (((1,), (1,)), ((), ()))
-
-
-def partial_kernel(cols, owners, share, factor, coeffs_t, out, half, mine, tiles):
+NY, NZ = 4, 16
+MESH = pl.DeviceIdType.MESH
+GROUPS = [[8]] + [[k, NZ - k] for k in range(7, 0, -1)] + [[0]]
+AHEAD, LAG = 2, 1
+
+
+def partial_kernel(cols, share, factor, coeffs_t, tiles, half, mine):
     m = pl.program_id(0)
     aux_count, _, entries, blk, _ = factor.shape
     occ = coeffs_t.shape[0]
     nb = cols.shape[0] // (aux_count * entries)
-    rows = out.shape[1]
+    rows = tiles.shape[1] // nb
     for q in range(aux_count):
         left, right = [], []
         for s in range(entries):
@@ -43,13 +47,112 @@
 
         lax.fori_loop(0, nb // 2, pair, 0)
 
-        def pick(k, carry):
-            pair_index = owners[k]
-            a, b = pair_index // nb, pair_index % nb
-            out[k] = tiles[b, pl.ds(pl.multiple_of(a * rows, rows), rows), :]
-            return carry
-
-        lax.fori_loop(0, nb * nb, pick, 0)
+
+def scatter_kernel(places, tiles, out, s_a, r_a, s_b, r_b, s_z, r_z, a_out, a_in, b_out, b_in, z_out, z_in):
+    me = lax.axis_index("aux")
+    y, z = me // NZ, me % NZ
+    own, rows = out.shape[0], out.shape[1]
+    size = own * rows
+    cut = (own + 1) // 2 * rows
+    y_to = [(y + 1) % NY * NZ + z, (y + NY - 1) % NY * NZ + z]
+    z_to = [y * NZ + (z + 1) % NZ, y * NZ + (z + NZ - 1) % NZ]
+
+    barrier = pltpu.get_barrier_semaphore()
+    for other in y_to + z_to:
+        pl.semaphore_signal(barrier, inc=1, device_id={"aux": other}, device_id_type=MESH)
+    pl.semaphore_wait(barrier, 4)
+
+    def chunk(up, d):
+        first = ((y + up) % NY * NZ + (z + d) % NZ) * own
+        picked = [
+            tiles[places[first + t]] for t in range(own)
+        ]
+        return jnp.concatenate(picked, axis=0)
+
+    def send(src, dst, out_sem, in_sem, other):
+        return pltpu.make_async_remote_copy(
+            src_ref=src, dst_ref=dst, send_sem=out_sem, recv_sem=in_sem,
+            device_id={"aux": other}, device_id_type=MESH,
+        )
+
+    def way(d):
+        return 0 if 1 <= d <= NZ // 2 else 1
+
+    def copy_a(d):
+        return send(s_a.at[d], r_a.at[d], a_out.at[d], a_in.at[d], y_to[way(d)])
+
+    def copy_b(w, d):
+        return send(s_b.at[w, d], r_b.at[w, d], b_out.at[w, d], b_in.at[w, d], y_to[w])
+
+    def copy_z(w, s):
+        if s == 0:
+            piece = pl.ds(0, cut) if w == 0 else pl.ds(cut, size - cut)
+            return send(s_z.at[w, 0, piece], r_z.at[w, 0, piece], z_out.at[w, 0], z_in.at[w, 0], z_to[w])
+        return send(s_z.at[w, s], r_z.at[w, s], z_out.at[w, s], z_in.at[w, s], z_to[w])
+
+    def first_hop(d):
+        s_a[d] = chunk(2, d)
+        copy_a(d).start()
+
+    def second_hop(d):
+        for w, up in ((0, 1), (1, NY - 1)):
+            part = chunk(up, d)
+            if way(d) == w:
+                copy_a(d).wait_recv()
+                part = part + r_a[d]
+            s_b[w, d] = part
+            copy_b(w, d).start()
+
+    def column(d):
+        copy_b(0, d).wait_recv()
+        copy_b(1, d).wait_recv()
+        return chunk(0, d) + r_b[0, d] + r_b[1, d]
+
+    def chain(s):
+        if s == 0:
+            part = column(NZ // 2)
+            s_z[0, 0, :cut] = part[:cut]
+            s_z[1, 0, cut:] = part[cut:]
+            copy_z(0, 0).start()
+            copy_z(1, 0).start()
+            return
+        if s == NZ // 2:
+            part = column(0)
+            for w in range(2):
+                copy_z(w, s - 1).wait_recv()
+            part = part + r_z[0, s - 1] + r_z[1, s - 1]
+            for t in range(own):
+                out[t] = part[t * rows : (t + 1) * rows]
+            return
+        for w, d in ((0, NZ // 2 - s), (1, NZ // 2 + s)):
+            part = column(d)
+            copy_z(w, s - 1).wait_recv()
+            if s == 1:
+                piece = slice(0, cut) if w == 0 else slice(cut, size)
+                came = part[piece] + r_z[w, 0, piece]
+                part = jnp.concatenate([came, part[cut:]] if w == 0 else [part[:cut], came], axis=0)
+            else:
+                part = part + r_z[w, s - 1]
+            s_z[w, s] = part
+            copy_z(w, s).start()
+
+    count = len(GROUPS)
+    for i in range(-AHEAD, count + LAG):
+        if i + AHEAD < count:
+            for d in GROUPS[i + AHEAD]:
+                first_hop(d)
+        if 0 <= i < count:
+            for d in GROUPS[i]:
+                second_hop(d)
+        if i - LAG >= 0:
+            chain(i - LAG)
+    for d in range(NZ):
+        copy_a(d).wait_send()
+        for w in range(2):
+            copy_b(w, d).wait_send()
+    for s in range(NZ // 2):
+        for w in range(2):
+            copy_z(w, s).wait_send()
 
 
 def shards(factor_tiles, tile_cols, coeffs, pair_owner):
@@ -57,29 +160,51 @@
     occ_ways = lax.axis_size("occ")
     rows = blk // occ_ways
     occ = coeffs.shape[1] * occ_ways
+    own = pair_owner.shape[0]
     coeffs_t = lax.all_gather(coeffs.T, "occ", axis=0, tiled=True)
-    owners = lax.all_gather(pair_owner, "aux", axis=0, tiled=True)
+    place = (pair_owner % nb) * nb + pair_owner // nb
+    places = lax.all_gather(place, "aux", axis=0, tiled=True)
     share = lax.axis_index("occ").astype(jnp.int32).reshape(1)
-    partial = pl.pallas_call(
+    tiles = pl.pallas_call(
         partial_kernel,
         grid_spec=pltpu.PrefetchScalarGridSpec(
-            num_scalar_prefetch=3,
+            num_scalar_prefetch=2,
             grid=(nb,),
             in_specs=[
                 pl.BlockSpec((aux_count, 1, entries, blk, blk), lambda m, *_: (0, m, 0, 0, 0)),
                 pl.BlockSpec((occ, nb * blk), lambda m, *_: (0, 0)),
             ],
-            out_specs=pl.BlockSpec((nb * nb, rows, blk), lambda m, *_: (0, 0, 0)),
+            out_specs=pl.BlockSpec((nb, nb * rows, blk), lambda m, *_: (0, 0, 0)),
             scratch_shapes=[
                 pltpu.VMEM((nb * blk, aux_count * occ), jnp.bfloat16),
                 pltpu.VMEM((nb * rows, aux_count * occ), jnp.bfloat16),
-                pltpu.VMEM((nb, nb * rows, blk), jnp.float32),
             ],
         ),
-        out_shape=jax.ShapeDtypeStruct((nb * nb, rows, blk), jnp.float32),
+        out_shape=jax.ShapeDtypeStruct((nb, nb * rows, blk), jnp.float32),
         compiler_params=pltpu.CompilerParams(vmem_limit_bytes=48 * 2**20),
-    )(tile_cols.reshape(-1), owners, share, factor_tiles, coeffs_t)
-    return lax.psum_scatter(partial, "aux", scatter_dimension=0, tiled=True)
+    )(tile_cols.reshape(-1), share, factor_tiles, coeffs_t)
+    piece = (own * rows, blk)
+    dma = pltpu.SemaphoreType.DMA
+    return pl.pallas_call(
+        scatter_kernel,
+        in_specs=[pl.BlockSpec(memory_space=pltpu.SMEM), pl.BlockSpec(memory_space=pltpu.VMEM)],
+        out_specs=pl.BlockSpec(memory_space=pltpu.VMEM),
+        out_shape=jax.ShapeDtypeStruct((own, rows, blk), jnp.float32),
+        scratch_shapes=[
+            pltpu.VMEM((NZ, *piece), jnp.float32),
+            pltpu.VMEM((NZ, *piece), jnp.float32),
+            pltpu.VMEM((2, NZ, *piece), jnp.float32),
+            pltpu.VMEM((2, NZ, *piece), jnp.float32),
+            pltpu.VMEM((2, NZ // 2, *piece), jnp.float32),
+            pltpu.VMEM((2, NZ // 2, *piece), jnp.float32),
+            dma((NZ,)), dma((NZ,)),
+            dma((2, NZ)), dma((2, NZ)),
+            dma((2, NZ // 2)), dma((2, NZ // 2)),
+        ],
+        compiler_params=pltpu.CompilerParams(
+            collective_id=0, has_side_effects=True, vmem_limit_bytes=48 * 2**20
+        ),
+    )(places, tiles.reshape(nb * nb, rows, blk))
 
 
 def solution(mesh):

time: 792 us -> 131 us (0.17); the launches traced: 782 us -> 129 us
  waiting for transfers between devices: 701 us -> 7.05 us
  Pallas kernels: 32.1 us -> 70.1 us
    reduce_scatter x1 -> x0, waiting for transfers between devices: 694 us -> none  [shards(): return lax.psum_scatter(partial, 'aux', scatter_dimension=0, tiled=True)]
    pallas_call x0 -> x1, Pallas kernels: none -> 47.8 us  [shards(): pl.pallas_call(scatter_kernel, in_specs=[pl.BlockSpec(memory_space=pltpu....]
    pallas_call x1, Pallas kernels: 32.1 us -> 22.3 us  [shards(): pl.pallas_call(partial_kernel, grid_spec=pltpu.PrefetchScalarGridSpec(num...]
  transfers between devices with their start and end apart: 2 -> 1, of which waited for: 2 -> 1; matrix products, arithmetic and copies ran while one was open for 0% -> 2% of each run, Pallas kernels for 0% -> 0%
where the time goes in v2:
time: 131 us; the launch traced here: 129 us
  Pallas kernels  70.1 us (54%)
  blocking collectives  30.2 us (23%)
  between operations  14.1 us (11%)
  waiting for transfers between devices  7.05 us (5%)
  local copies, waits for them, and re-layouts  6.52 us (5%)
    pallas_call x1, Pallas kernels, shards(): pl.pallas_call(scatter_kernel, in_specs=[pl.BlockSpec(memory_space=pltpu....  47.8 us
    unnamed x1, blocking collectives  30.2 us
    pallas_call x1, Pallas kernels, shards(): pl.pallas_call(partial_kernel, grid_spec=pltpu.PrefetchScalarGridSpec(num...  22.3 us
    unnamed x8, local copies, waits for them, and re-layouts  6.42 us
    all_gather x1, waiting for transfers between devices, shards(): coeffs_t = lax.all_gather(coeffs.T, 'occ', axis=0, tiled=True)  6.34 us
  transfers between devices with their start and end apart: 1, of which 1 were waited for; matrix products, arithmetic and copies ran while one was open for 2% of the time, Pallas kernels for 0%

profile of v2, /device:TPU:1, one launch (start us, length us, event | category | flops | bytes accessed | tf_op | source)
XLA Modules:
  0.0 128.7 jit_solution(12362086629154690202)
XLA Ops:
  6.5 0.0 all-gather.2.cloned.1.call-start
  6.5 0.7 all-gather.2.cloned.1.call-update
  7.3 0.8 copy.5
  8.0 0.1 reshape.9.cols
  8.1 1.3 dynamic-slice
  10.1 0.8 fusion.2
  10.9 30.2 %all-reduce.places = s32[576]{0:T(1024)S(1)} all-reduce(s32[576]{0:T(1024)S(1)} %fusion.2), channel_id=1, replica_groups=mesh['aux'=64,'occ'=8] {'aux'}, use_global_device_ids=true, to_apply=%add | all-reduce | flops 576 | bytes 4608
  41.0 6.3 %all-gather.2.cloned.1.call-done.coeffs_t = bf16[256,3072]{1,0:T(8,128)(2,1)} async-done(((bf16[32,3072]{1,0:T(8,128)(2,1)}), bf16[256,3072]{1,0:T(8,128)(2,1)}) %all-gather.2.cloned.1.call-update) | async-done | bytes 1572880 | tf_op jit(solution)/shard_map/all_gather | solution.py:164
  47.4 0.0 copy-start.1
  47.4 1.4 %copy-done.1 = bf16[256,3072]{1,0:T(8,128)(2,1)S(1)} copy-done((bf16[256,3072]{1,0:T(8,128)(2,1)S(1)}, bf16[256,3072]{1,0:T(8,128)(2,1)}, u32[]{:S(2)}) %copy-start.1) | copy-done | bytes 1572888
  48.8 22.3 %shard_map.46 = f32[24,384,128]{2,1,0:T(8,128)} custom-call(s32[192]{0:T(256)S(1)} %reshape.9.cols, s32[1]{0:T(128)} %bitcast.1.share, bf16[2,24,4,128,128]{4,3,2,1,0:T(8,128)(2,1)} %factor.1, bf16[256,3072]{1,0:T(8,128)(2,1)S(1)} %copy-done.1), custom_call_target="tpu_custom_call" | custom-call | tf_op jit(solution)/shard_map/pallas_call | solution.py:168
  71.1 0.0 copy-start
  71.1 2.3 %copy-done = f32[24,384,128]{2,1,0:T(8,128)S(1)} copy-done((f32[24,384,128]{2,1,0:T(8,128)S(1)}, f32[24,384,128]{2,1,0:T(8,128)}, u32[]{:S(2)}) %copy-start) | copy-done | bytes 4718616
  73.5 47.8 %shard_map.47 = f32[9,16,128]{2,1,0:T(8,128)S(1)} custom-call(s32[576]{0:T(1024)S(1)} %all-reduce.places, f32[576,16,128]{2,1,0:T(8,128)S(1)} %bitcast.4), custom_call_target="tpu_custom_call" | custom-call | tf_op jit(solution)/shard_map/pallas_call | solution.py:188
  121.2 0.6 copy.8
  (1 shorter events, 0.0 us)
Async XLA Ops:
  6.5 40.8 %all-gather.2.cloned.1.call-start = ((), (), s32[]{:S(2)}) async-start(), calls=%async_computation | async-start | bytes 1769472 | tf_op jit(solution)/shard_map/all_gather | solution.py:164
  47.4 1.4 %copy-start.1 = (bf16[256,3072]{1,0:T(8,128)(2,1)S(1)}, bf16[256,3072]{1,0:T(8,128)(2,1)}, u32[]{:S(2)}) copy-start(bf16[256,3072]{1,0:T(8,128)(2,1)} %all-gather.2.cloned.1.call-done.coeffs_t) | copy-start | bytes 4718596
  71.1 2.3 %copy-start = (f32[24,384,128]{2,1,0:T(8,128)S(1)}, f32[24,384,128]{2,1,0:T(8,128)}, u32[]{:S(2)}) copy-start(f32[24,384,128]{2,1,0:T(8,128)} %shard_map.46) | copy-start | bytes 14155780
Sparse Core Ops, SparseCore 0:
  9.5 37.8 all-gather.1

commit v3 on v0

v3 whole, which is shorter than its diff:
```python
import jax
import jax.numpy as jnp
from jax import lax
from jax.experimental import pallas as pl
from jax.experimental.pallas import tpu as pltpu
from jax.sharding import PartitionSpec as P

NT = (((1,), (1,)), ((), ()))
NX, NY, NZ = 4, 4, 16
MESH = pl.DeviceIdType.MESH
GROUPS = [[8]] + [[k, NZ - k] for k in range(7, 0, -1)] + [[0]]
AHEAD, LAG = 2, 1
STAGES = 4


def kernel(
    cols, owner, factor, coeffs_t, out,
    f_buf, c_all, half, mine, tiles, by_y, by_z, place,
    s_a, r_a, s_b, r_b, s_z, r_z,
    f_in, g_out, g_in, py_out, py_in, pz_out, pz_in, p_in,
    a_out, a_in, b_out, b_in, z_out, z_in,
):
    me, occ = lax.axis_index("aux"), lax.axis_index("occ")
    y, z = me // NZ, me % NZ
    x, core = occ // 2, occ % 2
    aux_count, nb, entries, blk, _ = f_buf.shape
    own, rows = out.shape[0], out.shape[1]
    share = coeffs_t.shape[0]
    all_occ = c_all.shape[1]
    size = own * rows
    cut = (own + 1) // 2 * rows
    step = nb // STAGES

    def up_y(k):
        return (y + k) % NY * NZ + z

    def up_z(k):
        return y * NZ + (z + k) % NZ

    def peer(dx, other_core=False):
        return (x + dx) % NX * 2 + (1 - core if other_core else core)

    loads = [
        pltpu.make_async_copy(
            factor.at[:, pl.ds(n * step, step)], f_buf.at[:, pl.ds(n * step, step)], f_in.at[n]
        )
        for n in range(STAGES)
    ]
    for load in loads:
        load.start()

    barrier = pltpu.get_barrier_semaphore()
    aux_peers = [up_y(k) for k in range(1, NY)] + [up_z(k) for k in range(1, NZ)]
    occ_peers = [peer(1), peer(NX - 1), peer(0, True)]
    for other in aux_peers:
        pl.semaphore_signal(barrier, inc=1, device_id={"aux": other}, device_id_type=MESH)
    for other in occ_peers:
        pl.semaphore_signal(barrier, inc=1, device_id={"occ": other}, device_id_type=MESH)

    for b in range(nb):
        c_all[b, pl.ds(pl.multiple_of(occ * share, share), share), :] = coeffs_t[
            :, b * blk : (b + 1) * blk
        ]
    lane = lax.broadcasted_iota(jnp.int32, (1, 128), 1)
    codes = jnp.zeros((1, 128), jnp.int32)
    for t in range(own):
        pair_index = owner[t]
        codes = jnp.where(lane == t, (pair_index % nb) * nb + pair_index // nb, codes)
    by_y[y] = codes
    pl.semaphore_wait(barrier, len(aux_peers) + len(occ_peers))

    def send(src, dst, out_sem, in_sem, **other):
        return pltpu.make_async_remote_copy(
            src_ref=src, dst_ref=dst, send_sem=out_sem, recv_sem=in_sem,
            device_id=other, device_id_type=MESH,
        )

    def block(who, part):
        lo, count = (0, nb) if part is None else (part * (nb // 2), nb // 2)
        return c_all.at[pl.ds(lo, count), pl.ds(pl.multiple_of(who * share, share), share)]

    def pass_on(n, who, part, to):
        ref = block(who, part)
        return send(ref, ref, g_out.at[n], g_in.at[n], occ=to)

    right, left, mate = peer(1), peer(NX - 1), peer(0, True)
    moves = [
        (occ, peer(-1 + NX), 0, right),
        (occ, peer(1), 1, left),
        (occ, peer(-1 + NX), 1, right),
        (occ, peer(1), 0, left),
        (peer(-1 + NX), peer(2), 0, right),
        (peer(1), peer(2), 1, left),
        (occ, mate, None, mate),
        (peer(-1 + NX), peer(-1 + NX, True), 0, mate),
        (peer(1), peer(1, True), 1, mate),
        (peer(-1 + NX), peer(-1 + NX, True), 1, mate),
        (peer(1), peer(1, True), 0, mate),
        (peer(2), peer(2, True), 0, mate),
        (peer(2), peer(2, True), 1, mate),
    ]

    def go(n):
        pass_on(n, moves[n][0], moves[n][2], moves[n][3]).start()

    def got(n):
        pass_on(n, moves[n][1], moves[n][2], moves[n][3]).wait_recv()

    def place_y(k, row):
        return send(by_y.at[row], by_y.at[row], py_out.at[k - 1], py_in.at[k - 1], aux=up_y(k))

    def place_z(k, row):
        return send(by_z.at[row], by_z.at[row], pz_out.at[k - 1], pz_in.at[k - 1], aux=up_z(k))

    for n in (0, 1, 2, 3, 6):
        go(n)
    for k in range(1, NY):
        place_y(k, y).start()
    for n, then in ((0, (4, 7)), (1, (5, 8)), (2, (9,)), (3, (10,))):
        got(n)
        for nxt in then:
            go(nxt)
    for k in range(1, NY):
        place_y(k, (y + NY - k) % NY).wait_recv()
    by_z[z] = by_y[...]
    for k in range(1, NZ):
        place_z(k, z).start()
    for n, nxt in ((4, 11), (5, 12)):
        got(n)
        go(nxt)
    for n in range(6, 13):
        got(n)

    for n in range(STAGES):
        loads[n].wait()

        def one(m, carry):
            for q in range(aux_count):
                lhs = jnp.concatenate([f_buf[q, m, s] for s in range(entries)], axis=1)
                rhs = jnp.concatenate([c_all[cols[q, s, m]] for s in range(entries)], axis=1)
                done = lax.dot_general(lhs, rhs, NT, preferred_element_type=jnp.float32)
                half[m, :, q * all_occ : (q + 1) * all_occ] = done.astype(jnp.bfloat16)
            mine[m] = half[m, pl.ds(pl.multiple_of(occ * rows, rows), rows), :]
            return carry

        lax.fori_loop(n * step, (n + 1) * step, one, 0, unroll=2)

    def pair(p, carry):
        lhs = mine[...].reshape(nb * rows, aux_count * all_occ)
        rhs = half[pl.ds(2 * p, 2)].reshape(2 * blk, aux_count * all_occ)
        prod = lax.dot_general(lhs, rhs, NT, preferred_element_type=jnp.float32)
        tiles[pl.ds(2 * p * nb, nb)] = prod[:, :blk].reshape(nb, rows, blk)
        tiles[pl.ds((2 * p + 1) * nb, nb)] = prod[:, blk:].reshape(nb, rows, blk)
        return carry

    lax.fori_loop(0, nb // 2, pair, 0, unroll=2)

    for k in range(1, NZ):
        place_z(k, (z + NZ - k) % NZ).wait_recv()
    fetch = pltpu.make_async_copy(by_z, place, p_in.at[0])
    fetch.start()
    fetch.wait()

    def chunk(up, d):
        yy, zz = (y + up) % NY, (z + d) % NZ
        return jnp.concatenate([tiles[place[zz, yy, 0, t]] for t in range(own)], axis=0)

    def encode(part):
        lead = part.reshape(part.shape[0] // 8, 8, blk)
        top = jnp.max(jnp.abs(lead), axis=0)
        power = jnp.ceil(jnp.log2(jnp.maximum(top, 1e-33)))
        scaled = jnp.round(lead * jnp.exp2(15.0 - power)[None])
        fixed = jnp.clip(scaled, -32767.0, 32767.0).astype(jnp.int32).reshape(part.shape)
        tail = power.astype(jnp.int32)
        return jnp.concatenate([fixed, tail, tail], axis=0).astype(jnp.int16)

    def decode(got_piece):
        wide = got_piece.astype(jnp.int32).astype(jnp.float32)
        n = got_piece.shape[0] - 16
        lead = wide[:n].reshape(n // 8, 8, blk)
        return (lead * jnp.exp2(wide[n : n + 8] - 15.0)[None]).reshape(n, blk)

    def way(d):
        return 0 if 1 <= d <= NZ // 2 else 1

    y_to = [up_y(1), up_y(NY - 1)]
    z_to = [up_z(1), up_z(NZ - 1)]

    def copy_a(d):
        return send(s_a.at[d], r_a.at[d], a_out.at[d], a_in.at[d], aux=y_to[way(d)])

    def copy_b(w, d):
        return send(s_b.at[w, d], r_b.at[w, d], b_out.at[w, d], b_in.at[w, d], aux=y_to[w])

    ends = [cut + 16, size - cut + 16]

    def copy_z(w, s):
        piece = pl.ds(0, ends[w] if s == 0 else size + 16)
        return send(s_z.at[w, s, piece], r_z.at[w, s, piece], z_out.at[w, s], z_in.at[w, s], aux=z_to[w])

    def first_hop(d):
        s_a[d] = encode(chunk(2, d))
        copy_a(d).start()

    def second_hop(d):
        for w, up in ((0, 1), (1, NY - 1)):
            part = chunk(up, d)
            if way(d) == w:
                copy_a(d).wait_recv()
                part = part + decode(r_a[d])
            s_b[w, d] = encode(part)
            copy_b(w, d).start()

    def column(d):
        copy_b(0, d).wait_recv()
        copy_b(1, d).wait_recv()
        return chunk(0, d) + decode(r_b[0, d]) + decode(r_b[1, d])

    def chain(s):
        if s == 0:
            part = column(NZ // 2)
            s_z[0, 0, : ends[0]] = encode(part[:cut])
            s_z[1, 0, : ends[1]] = encode(part[cut:])
            copy_z(0, 0).start()
            copy_z(1, 0).start()
            return
        if s == NZ // 2:
            part = column(0)
            for w in range(2):
                copy_z(w, s - 1).wait_recv()
            part = part + decode(r_z[0, s - 1]) + decode(r_z[1, s - 1])
            out[...] = part.reshape(own, rows, blk)
            return
        for w, d in ((0, NZ // 2 - s), (1, NZ // 2 + s)):
            part = column(d)
            copy_z(w, s - 1).wait_recv()
            if s == 1:
                came = decode(r_z[w, 0, : ends[w]])
                if w == 0:
                    part = jnp.concatenate([part[:cut] + came, part[cut:]], axis=0)
                else:
                    part = jnp.concatenate([part[:cut], part[cut:] + came], axis=0)
            else:
                part = part + decode(r_z[w, s - 1])
            s_z[w, s] = encode(part)
            copy_z(w, s).start()

    count = len(GROUPS)
    for i in range(-AHEAD, count + LAG):
        if i + AHEAD < count:
            for d in GROUPS[i + AHEAD]:
                first_hop(d)
        if 0 <= i < count:
            for d in GROUPS[i]:
                second_hop(d)
        if i - LAG >= 0:
            chain(i - LAG)

    for n in range(13):
        pass_on(n, moves[n][0], moves[n][2], moves[n][3]).wait_send()
    for k in range(1, NY):
        place_y(k, y).wait_send()
    for k in range(1, NZ):
        place_z(k, z).wait_send()
    for d in range(NZ):
        copy_a(d).wait_send()
        for w in range(2):
            copy_b(w, d).wait_send()
    for s in range(NZ // 2):
        for w in range(2):
            copy_z(w, s).wait_send()


def shards(factor_tiles, tile_cols, coeffs, pair_owner):
    aux_count, nb, entries, blk, _ = factor_tiles.shape
    occ_ways = lax.axis_size("occ")
    rows = blk // occ_ways
    occ = coeffs.shape[1] * occ_ways
    own = pair_owner.shape[0]
    piece = (own * rows + 16, blk)
    dma = pltpu.SemaphoreType.DMA
    smem = pl.BlockSpec(memory_space=pltpu.SMEM)
    vmem = pl.BlockSpec(memory_space=pltpu.VMEM)
    return pl.pallas_call(
        kernel,
        in_specs=[smem, smem, pl.BlockSpec(memory_space=pl.ANY), vmem],
        out_specs=vmem,
        out_shape=jax.ShapeDtypeStruct((own, rows, blk), jnp.float32),
        scratch_shapes=[
            pltpu.VMEM(factor_tiles.shape, jnp.bfloat16),
            pltpu.VMEM((nb, occ, blk), jnp.bfloat16),
            pltpu.VMEM((nb, blk, aux_count * occ), jnp.bfloat16),
            pltpu.VMEM((nb, rows, aux_count * occ), jnp.bfloat16),
            pltpu.VMEM((nb * nb, rows, blk), jnp.float32),
            pltpu.VMEM((NY, 1, 128), jnp.int32),
            pltpu.VMEM((NZ, NY, 1, 128), jnp.int32),
            pltpu.SMEM((NZ, NY, 1, 128), jnp.int32),
            pltpu.VMEM((NZ, *piece), jnp.int16),
            pltpu.VMEM((NZ, *piece), jnp.int16),
            pltpu.VMEM((2, NZ, *piece), jnp.int16),
            pltpu.VMEM((2, NZ, *piece), jnp.int16),
            pltpu.VMEM((2, NZ // 2, *piece), jnp.int16),
            pltpu.VMEM((2, NZ // 2, *piece), jnp.int16),
            dma((STAGES,)),
            dma((13,)), dma((13,)),
            dma((NY - 1,)), dma((NY - 1,)),
            dma((NZ - 1,)), dma((NZ - 1,)),
            dma((1,)),
            dma((NZ,)), dma((NZ,)),
            dma((2, NZ)), dma((2, NZ)),
            dma((2, NZ // 2)), dma((2, NZ // 2)),
        ],
        compiler_params=pltpu.CompilerParams(
            collective_id=0, has_side_effects=True, vmem_limit_bytes=48 * 2**20
        ),
    )(jnp.transpose(tile_cols, (0, 2, 1)), pair_owner, factor_tiles, coeffs.T)


def solution(mesh):
    placed = (P("aux", None, None, None, None), P("aux", None, None), P(None, "occ"), P("aux"))
    return jax.shard_map(
        shards, mesh=mesh, in_specs=placed, out_specs=P("aux", "occ", None), check_vma=False
    )
```

time: 415 us -> 73 us (0.18)
  the two profiles are of different devices: /device:TPU:1 before, /device:TPU:32 now
where the time goes in v3:
time: 73 us; the launch traced here: 72.8 us
  Pallas kernels  69.9 us (96%)
  local copies, waits for them, and re-layouts  2.9 us (4%)
    pallas_call x1, Pallas kernels, shards(): pl.pallas_call(kernel, in_specs=[smem, smem, pl.BlockSpec(memory_space=pl...  69.9 us
    unnamed x7, local copies, waits for them, and re-layouts  2.9 us

profile of v3, /device:TPU:32, one launch (start us, length us, event | category | flops | bytes accessed | tf_op | source)
XLA Modules:
  0.0 72.8 jit_solution(17373306748799412361)
XLA Ops:
  0.0 0.0 copy-start
  0.0 0.9 %copy-done = bf16[3072,32]{0,1:T(8,128)(2,1)S(1)} copy-done((bf16[3072,32]{0,1:T(8,128)(2,1)S(1)}, bf16[3072,32]{0,1:T(8,128)(2,1)}, u32[]{:S(2)}) %copy-start) | copy-done | bytes 196632
  0.9 0.0 copy-start.1
  0.9 0.7 copy-done.1
  1.6 0.0 copy-start.2
  1.6 0.7 copy-done.2
  2.3 69.9 %shard_map.46 = f32[9,16,128]{2,1,0:T(8,128)S(1)} custom-call(s32[2,4,24]{2,1,0:T(4,128)S(1)} %bitcast.3, s32[9]{0:T(128)S(1)} %copy-done.2, bf16[2,24,4,128,128]{4,3,2,1,0:T(8,128)(2,1)} %factor.1, bf16[32,3072]{1,0:T(8,128)(2,1)S(1)} %bitcast.2), custom_call_target="tpu_custom_call" | custom-call | tf_op jit(solution)/shard_map/pallas_call | solution.py:284
  72.2 0.6 copy.6
Async XLA Ops:
  0.0 0.9 %copy-start = (bf16[3072,32]{0,1:T(8,128)(2,1)S(1)}, bf16[3072,32]{0,1:T(8,128)(2,1)}, u32[]{:S(2)}) copy-start(bf16[3072,32]{0,1:T(8,128)(2,1)} %param.6) | copy-start | bytes 589828
  0.9 0.7 copy-start.1
  1.6 0.7 copy-start.2

commit v4 on v3

--- a/solution.py
+++ b/solution.py
@@ -8,17 +8,18 @@
 NT = (((1,), (1,)), ((), ()))
 NX, NY, NZ = 4, 4, 16
 MESH = pl.DeviceIdType.MESH
-GROUPS = [[8]] + [[k, NZ - k] for k in range(7, 0, -1)] + [[0]]
-AHEAD, LAG = 2, 1
+ORDER = [8, 7, 9, 6, 10, 5, 11, 4, 12, 3, 13, 2, 14, 0]
+AHEAD, LAG, MID_AT, MERGE_AT = 6, 3, 10, -3
+MESSAGES = 76
 STAGES = 4
 
 
 def kernel(
-    cols, owner, factor, coeffs_t, out,
-    f_buf, c_all, half, mine, tiles, by_y, by_z, place,
-    s_a, r_a, s_b, r_b, s_z, r_z,
-    f_in, g_out, g_in, py_out, py_in, pz_out, pz_in, p_in,
-    a_out, a_in, b_out, b_in, z_out, z_in,
+    cols_in, owner_in, factor, coeffs_in, out,
+    cols, owner, coeffs_t, f_buf, c_all, half, mine, tiles, by_y, by_z, place,
+    s_msg, r_msg, s_scale, r_scale, kept, merged,
+    arg_in, f_in, g_out, g_in, py_out, py_in, pz_out, pz_in, p_in,
+    m_out, m_in, c_out, c_in,
 ):
     me, occ = lax.axis_index("aux"), lax.axis_index("occ")
     y, z = me // NZ, me % NZ
@@ -27,8 +28,6 @@
     own, rows = out.shape[0], out.shape[1]
     share = coeffs_t.shape[0]
     all_occ = c_all.shape[1]
-    size = own * rows
-    cut = (own + 1) // 2 * rows
     step = nb // STAGES
 
     def up_y(k):
@@ -40,6 +39,12 @@
     def peer(dx, other_core=False):
         return (x + dx) % NX * 2 + (1 - core if other_core else core)
 
+    args = [
+        pltpu.make_async_copy(src, dst, arg_in.at[n])
+        for n, (src, dst) in enumerate(((coeffs_in, coeffs_t), (owner_in, owner), (cols_in, cols)))
+    ]
+    for arg in args:
+        arg.start()
     loads = [
         pltpu.make_async_copy(
             factor.at[:, pl.ds(n * step, step)], f_buf.at[:, pl.ds(n * step, step)], f_in.at[n]
@@ -57,6 +62,8 @@
     for other in occ_peers:
         pl.semaphore_signal(barrier, inc=1, device_id={"occ": other}, device_id_type=MESH)
 
+    for arg in args:
+        arg.wait()
     for b in range(nb):
         c_all[b, pl.ds(pl.multiple_of(occ * share, share), share), :] = coeffs_t[
             :, b * blk : (b + 1) * blk
@@ -161,114 +168,119 @@
     fetch.start()
     fetch.wait()
 
+    def post(n, part, axis_to):
+        top = jnp.maximum(jnp.max(jnp.abs(part), axis=0, keepdims=True), 1e-30)
+        count = part.shape[0]
+        s_msg[n, :count] = jnp.round(part * (32767.0 / top)).astype(jnp.int32).astype(jnp.int16)
+        s_scale[n] = top * (1.0 / 32767.0)
+        sent.append((n, count, axis_to))
+        for copy in copies(n, count, axis_to):
+            copy.start()
+
+    def copies(n, count, axis_to):
+        piece = pl.ds(0, count)
+        return (
+            send(s_msg.at[n, piece], r_msg.at[n, piece], m_out.at[n], m_in.at[n], aux=axis_to),
+            send(s_scale.at[n], r_scale.at[n], c_out.at[n], c_in.at[n], aux=axis_to),
+        )
+
+    def take(n, count):
+        for copy in copies(n, count, y_to[0]):
+            copy.wait_recv()
+        return r_msg[n, :count].astype(jnp.int32).astype(jnp.float32) * r_scale[n]
+
+    sent = []
+    y_to = [up_y(1), up_y(NY - 1)]
+    z_to = [up_z(1), up_z(NZ - 1)]
+    far_to = [up_z(4), up_z(NZ - 4)]
+    size, cut = own * rows, (own + 1) // 2 * rows
+    halves = (cut, size - cut)
+    msg_a, msg_b, msg_n, msg_q, msg_e, msg_m = 0, 16, 48, 64, 66, 68
+
     def chunk(up, d):
         yy, zz = (y + up) % NY, (z + d) % NZ
         return jnp.concatenate([tiles[place[zz, yy, 0, t]] for t in range(own)], axis=0)
 
-    def encode(part):
-        lead = part.reshape(part.shape[0] // 8, 8, blk)
-        top = jnp.max(jnp.abs(lead), axis=0)
-        power = jnp.ceil(jnp.log2(jnp.maximum(top, 1e-33)))
-        scaled = jnp.round(lead * jnp.exp2(15.0 - power)[None])
-        fixed = jnp.clip(scaled, -32767.0, 32767.0).astype(jnp.int32).reshape(part.shape)
-        tail = power.astype(jnp.int32)
-        return jnp.concatenate([fixed, tail, tail], axis=0).astype(jnp.int16)
-
-    def decode(got_piece):
-        wide = got_piece.astype(jnp.int32).astype(jnp.float32)
-        n = got_piece.shape[0] - 16
-        lead = wide[:n].reshape(n // 8, 8, blk)
-        return (lead * jnp.exp2(wide[n : n + 8] - 15.0)[None]).reshape(n, blk)
+    def near(up, d):
+        return merged[up] if d == 0 else chunk(up, d)
 
     def way(d):
         return 0 if 1 <= d <= NZ // 2 else 1
 
-    y_to = [up_y(1), up_y(NY - 1)]
-    z_to = [up_z(1), up_z(NZ - 1)]
-
-    def copy_a(d):
-        return send(s_a.at[d], r_a.at[d], a_out.at[d], a_in.at[d], aux=y_to[way(d)])
-
-    def copy_b(w, d):
-        return send(s_b.at[w, d], r_b.at[w, d], b_out.at[w, d], b_in.at[w, d], aux=y_to[w])
-
-    ends = [cut + 16, size - cut + 16]
-
-    def copy_z(w, s):
-        piece = pl.ds(0, ends[w] if s == 0 else size + 16)
-        return send(s_z.at[w, s, piece], r_z.at[w, s, piece], z_out.at[w, s], z_in.at[w, s], aux=z_to[w])
-
     def first_hop(d):
-        s_a[d] = encode(chunk(2, d))
-        copy_a(d).start()
+        post(msg_a + d, near(2, d), y_to[way(d)])
 
     def second_hop(d):
         for w, up in ((0, 1), (1, NY - 1)):
-            part = chunk(up, d)
+            part = near(up, d)
             if way(d) == w:
-                copy_a(d).wait_recv()
-                part = part + decode(r_a[d])
-            s_b[w, d] = encode(part)
-            copy_b(w, d).start()
+                part = part + take(msg_a + d, size)
+            post(msg_b + w * NZ + d, part, y_to[w])
 
     def column(d):
-        copy_b(0, d).wait_recv()
-        copy_b(1, d).wait_recv()
-        return chunk(0, d) + decode(r_b[0, d]) + decode(r_b[1, d])
-
-    def chain(s):
-        if s == 0:
-            part = column(NZ // 2)
-            s_z[0, 0, : ends[0]] = encode(part[:cut])
-            s_z[1, 0, : ends[1]] = encode(part[cut:])
-            copy_z(0, 0).start()
-            copy_z(1, 0).start()
-            return
-        if s == NZ // 2:
-            part = column(0)
-            for w in range(2):
-                copy_z(w, s - 1).wait_recv()
-            part = part + decode(r_z[0, s - 1]) + decode(r_z[1, s - 1])
-            out[...] = part.reshape(own, rows, blk)
-            return
-        for w, d in ((0, NZ // 2 - s), (1, NZ // 2 + s)):
-            part = column(d)
-            copy_z(w, s - 1).wait_recv()
-            if s == 1:
-                came = decode(r_z[w, 0, : ends[w]])
-                if w == 0:
-                    part = jnp.concatenate([part[:cut] + came, part[cut:]], axis=0)
-                else:
-                    part = jnp.concatenate([part[:cut], part[cut:] + came], axis=0)
-            else:
-                part = part + decode(r_z[w, s - 1])
-            s_z[w, s] = encode(part)
-            copy_z(w, s).start()
-
-    count = len(GROUPS)
+        part = near(0, d) + take(msg_b + d, size) + take(msg_b + NZ + d, size)
+        if d % 4 == 0 and d != 8:
+            kept[d // 4] = part
+        elif d == 8:
+            post(msg_q, part[:cut], far_to[0])
+            post(msg_q + 1, part[cut:], far_to[1])
+        else:
+            hop = d % 4 if d < 8 else -(-d % 4)
+            post(msg_n + d, part, up_z(hop % NZ))
+
+    def merge_out():
+        for up in (2, 1, 3, 0):
+            for w, d in ((0, 1), (1, NZ - 1)):
+                post(msg_m + w * NY + up, chunk(up, d), z_to[w])
+
+    def merge_in():
+        for up in (2, 1, 3, 0):
+            merged[up] = chunk(up, 0) + take(msg_m + up, size) + take(msg_m + NY + up, size)
+
+    def collect(d, others):
+        part = kept[d // 4]
+        for o in others:
+            part = part + take(msg_n + o, size)
+        return part
+
+    def collect_mid(w):
+        part = collect(*((4, (7, 6, 5)), (12, (9, 10, 11)))[w])
+        came = take(msg_q + w, halves[w])
+        if w == 0:
+            part = jnp.concatenate([part[:cut] + came, part[cut:]], axis=0)
+        else:
+            part = jnp.concatenate([part[:cut], part[cut:] + came], axis=0)
+        post(msg_e + w, part, far_to[w])
+
+    count = len(ORDER)
     for i in range(-AHEAD, count + LAG):
         if i + AHEAD < count:
-            for d in GROUPS[i + AHEAD]:
-                first_hop(d)
+            if ORDER[i + AHEAD] == 0:
+                merge_in()
+            first_hop(ORDER[i + AHEAD])
+        if i == MERGE_AT:
+            merge_out()
         if 0 <= i < count:
-            for d in GROUPS[i]:
-                second_hop(d)
+            second_hop(ORDER[i])
         if i - LAG >= 0:
-            chain(i - LAG)
-
+            column(ORDER[i - LAG])
+        if i - LAG == MID_AT:
+            collect_mid(0)
+            collect_mid(1)
+    part = collect(0, (3, 13, 2, 14))
+    for w in range(2):
+        part = part + take(msg_e + w, size)
+    out[...] = part.reshape(own, rows, blk)
+
+    for n, count, axis_to in sent:
+        for copy in copies(n, count, axis_to):
+            copy.wait_send()
     for n in range(13):
         pass_on(n, moves[n][0], moves[n][2], moves[n][3]).wait_send()
     for k in range(1, NY):
         place_y(k, y).wait_send()
     for k in range(1, NZ):
         place_z(k, z).wait_send()
-    for d in range(NZ):
-        copy_a(d).wait_send()
-        for w in range(2):
-            copy_b(w, d).wait_send()
-    for s in range(NZ // 2):
-        for w in range(2):
-            copy_z(w, s).wait_send()
 
 
 def shards(factor_tiles, tile_cols, coeffs, pair_owner):
@@ -277,16 +289,17 @@
     rows = blk // occ_ways
     occ = coeffs.shape[1] * occ_ways
     own = pair_owner.shape[0]
-    piece = (own * rows + 16, blk)
     dma = pltpu.SemaphoreType.DMA
-    smem = pl.BlockSpec(memory_space=pltpu.SMEM)
     vmem = pl.BlockSpec(memory_space=pltpu.VMEM)
     return pl.pallas_call(
         kernel,
-        in_specs=[smem, smem, pl.BlockSpec(memory_space=pl.ANY), vmem],
+        in_specs=[pl.BlockSpec(memory_space=pltpu.HBM)] * 4,
         out_specs=vmem,
         out_shape=jax.ShapeDtypeStruct((own, rows, blk), jnp.float32),
         scratch_shapes=[
+            pltpu.SMEM((aux_count, entries, nb), jnp.int32),
+            pltpu.SMEM((own,), jnp.int32),
+            pltpu.VMEM(coeffs.shape[::-1], jnp.bfloat16),
             pltpu.VMEM(factor_tiles.shape, jnp.bfloat16),
             pltpu.VMEM((nb, occ, blk), jnp.bfloat16),
             pltpu.VMEM((nb, blk, aux_count * occ), jnp.bfloat16),
@@ -295,23 +308,23 @@
             pltpu.VMEM((NY, 1, 128), jnp.int32),
             pltpu.VMEM((NZ, NY, 1, 128), jnp.int32),
             pltpu.SMEM((NZ, NY, 1, 128), jnp.int32),
-            pltpu.VMEM((NZ, *piece), jnp.int16),
-            pltpu.VMEM((NZ, *piece), jnp.int16),
-            pltpu.VMEM((2, NZ, *piece), jnp.int16),
-            pltpu.VMEM((2, NZ, *piece), jnp.int16),
-            pltpu.VMEM((2, NZ // 2, *piece), jnp.int16),
-            pltpu.VMEM((2, NZ // 2, *piece), jnp.int16),
+            pltpu.VMEM((MESSAGES, own * rows, blk), jnp.int16),
+            pltpu.VMEM((MESSAGES, own * rows, blk), jnp.int16),
+            pltpu.VMEM((MESSAGES, 1, blk), jnp.float32),
+            pltpu.VMEM((MESSAGES, 1, blk), jnp.float32),
+            pltpu.VMEM((4, own * rows, blk), jnp.float32),
+            pltpu.VMEM((NY, own * rows, blk), jnp.float32),
+            dma((3,)),
             dma((STAGES,)),
             dma((13,)), dma((13,)),
             dma((NY - 1,)), dma((NY - 1,)),
             dma((NZ - 1,)), dma((NZ - 1,)),
             dma((1,)),
-            dma((NZ,)), dma((NZ,)),
-            dma((2, NZ)), dma((2, NZ)),
-            dma((2, NZ // 2)), dma((2, NZ // 2)),
+            dma((MESSAGES,)), dma((MESSAGES,)),
+            dma((MESSAGES,)), dma((MESSAGES,)),
         ],
         compiler_params=pltpu.CompilerParams(
-            collective_id=0, has_side_effects=True, vmem_limit_bytes=48 * 2**20
+            collective_id=0, has_side_effects=True, vmem_limit_bytes=61 * 2**20
         ),
     )(jnp.transpose(tile_cols, (0, 2, 1)), pair_owner, factor_tiles, coeffs.T)
 

time: 73 us -> 69.2 us (0.948)
  the two profiles are of different devices: /device:TPU:32 before, /device:TPU:1 now
where the time goes in v4:
time: 69.2 us; the launch traced here: 68.6 us
  Pallas kernels  67.1 us (97%)
  local copies, waits for them, and re-layouts  1.52 us (2%)
    pallas_call x1, Pallas kernels, shards(): pl.pallas_call(kernel, in_specs=[pl.BlockSpec(memory_space=pltpu.HBM)] *...  67.1 us
    unnamed x1, local copies, waits for them, and re-layouts  1.52 us

profile of v4, /device:TPU:1, one launch (start us, length us, event | category | flops | bytes accessed | tf_op | source)
XLA Modules:
  0.0 68.6 jit_solution(6054152305673099948)
XLA Ops:
  0.0 67.1 %shard_map.46 = f32[9,16,128]{2,1,0:T(8,128)} custom-call(s32[2,4,24]{2,1,0:T(4,128)} %bitcast.3, s32[9]{0:T(128)} %owner_in.1, bf16[2,24,4,128,128]{4,3,2,1,0:T(8,128)(2,1)} %factor.1, bf16[32,3072]{1,0:T(8,128)(2,1)} %bitcast.2), custom_call_target="tpu_custom_call" | custom-call | tf_op jit(solution)/shard_map/pallas_call | solution.py:294
  67.1 1.5 %copy.6 = f32[9,16,128]{2,1,0:T(8,128)} copy(f32[9,16,128]{2,1,0:T(8,128)} %shard_map.46) | data formatting | bytes 147456

commit v5 on v4

--- a/solution.py
+++ b/solution.py
@@ -9,14 +9,14 @@
 NX, NY, NZ = 4, 4, 16
 MESH = pl.DeviceIdType.MESH
 ORDER = [8, 7, 9, 6, 10, 5, 11, 4, 12, 3, 13, 2, 14, 0]
-AHEAD, LAG, MID_AT, MERGE_AT = 6, 3, 10, -3
+AHEAD, LAG, MID_AT, MERGE_AT, LATE_BY = 13, 7, 11, -9, 6
 MESSAGES = 76
 STAGES = 4
 
 
 def kernel(
     cols_in, owner_in, factor, coeffs_in, out,
-    cols, owner, coeffs_t, f_buf, c_all, half, mine, tiles, by_y, by_z, place,
+    cols, owner, coeffs_t, f_buf, c_near, c_far, half, mine, tiles, by_y, by_z, place,
     s_msg, r_msg, s_scale, r_scale, kept, merged,
     arg_in, f_in, g_out, g_in, py_out, py_in, pz_out, pz_in, p_in,
     m_out, m_in, c_out, c_in,
@@ -27,7 +27,8 @@
     aux_count, nb, entries, blk, _ = f_buf.shape
     own, rows = out.shape[0], out.shape[1]
     share = coeffs_t.shape[0]
-    all_occ = c_all.shape[1]
+    lanes = c_near.shape[1]
+    all_occ = 2 * lanes
     step = nb // STAGES
 
     def up_y(k):
@@ -65,9 +66,7 @@
     for arg in args:
         arg.wait()
     for b in range(nb):
-        c_all[b, pl.ds(pl.multiple_of(occ * share, share), share), :] = coeffs_t[
-            :, b * blk : (b + 1) * blk
-        ]
+        c_near[b, :share, :] = coeffs_t[:, b * blk : (b + 1) * blk]
     lane = lax.broadcasted_iota(jnp.int32, (1, 128), 1)
     codes = jnp.zeros((1, 128), jnp.int32)
     for t in range(own):
@@ -82,36 +81,37 @@
             device_id=other, device_id_type=MESH,
         )
 
-    def block(who, part):
+    def block(slot, part):
         lo, count = (0, nb) if part is None else (part * (nb // 2), nb // 2)
-        return c_all.at[pl.ds(lo, count), pl.ds(pl.multiple_of(who * share, share), share)]
-
-    def pass_on(n, who, part, to):
-        ref = block(who, part)
-        return send(ref, ref, g_out.at[n], g_in.at[n], occ=to)
+        ref, at = (c_near, slot) if slot < 4 else (c_far, slot - 4)
+        return ref.at[pl.ds(lo, count), pl.ds(at * share, share)]
+
+    def pass_on(n):
+        src, dst, part, to = moves[n]
+        return send(block(src, part), block(dst, part), g_out.at[n], g_in.at[n], occ=to)
 
     right, left, mate = peer(1), peer(NX - 1), peer(0, True)
     moves = [
-        (occ, peer(-1 + NX), 0, right),
-        (occ, peer(1), 1, left),
-        (occ, peer(-1 + NX), 1, right),
-        (occ, peer(1), 0, left),
-        (peer(-1 + NX), peer(2), 0, right),
-        (peer(1), peer(2), 1, left),
-        (occ, mate, None, mate),
-        (peer(-1 + NX), peer(-1 + NX, True), 0, mate),
-        (peer(1), peer(1, True), 1, mate),
-        (peer(-1 + NX), peer(-1 + NX, True), 1, mate),
-        (peer(1), peer(1, True), 0, mate),
-        (peer(2), peer(2, True), 0, mate),
-        (peer(2), peer(2, True), 1, mate),
+        (0, 2, 0, right),
+        (0, 4, 1, left),
+        (0, 2, 1, right),
+        (0, 4, 0, left),
+        (2, 6, 0, right),
+        (4, 6, 1, left),
+        (0, 1, None, mate),
+        (2, 3, 0, mate),
+        (4, 5, 1, mate),
+        (2, 3, 1, mate),
+        (4, 5, 0, mate),
+        (6, 7, 0, mate),
+        (6, 7, 1, mate),
     ]
 
     def go(n):
-        pass_on(n, moves[n][0], moves[n][2], moves[n][3]).start()
+        pass_on(n).start()
 
     def got(n):
-        pass_on(n, moves[n][1], moves[n][2], moves[n][3]).wait_recv()
+        pass_on(n).wait_recv()
 
     def place_y(k, row):
         return send(by_y.at[row], by_y.at[row], py_out.at[k - 1], py_in.at[k - 1], aux=up_y(k))
@@ -132,25 +132,38 @@
     by_z[z] = by_y[...]
     for k in range(1, NZ):
         place_z(k, z).start()
+    def halves_of(first, last, side, finish):
+        def one(m, carry):
+            for q in range(aux_count):
+                lhs = jnp.concatenate([f_buf[q, m, s] for s in range(entries)], axis=1)
+                blocks = c_far if side else c_near
+                rhs = jnp.concatenate([blocks[cols[q, s, m]] for s in range(entries)], axis=1)
+                done = lax.dot_general(lhs, rhs, NT, preferred_element_type=jnp.float32)
+                at = q * all_occ + side * lanes
+                half[m, :, at : at + lanes] = done.astype(jnp.bfloat16)
+            if finish:
+                mine[m] = half[m, pl.ds(pl.multiple_of(occ * rows, rows), rows), :]
+            return carry
+
+        lax.fori_loop(first, last, one, 0, unroll=6)
+
+    for load in loads:
+        load.wait()
+    for n in (6, 7, 9):
+        got(n)
+    halves_of(0, nb // 4, 0, False)
     for n, nxt in ((4, 11), (5, 12)):
         got(n)
         go(nxt)
-    for n in range(6, 13):
+    halves_of(nb // 4, nb, 0, False)
+    for n in (8, 10, 11, 12):
         got(n)
-
-    for n in range(STAGES):
-        loads[n].wait()
-
-        def one(m, carry):
-            for q in range(aux_count):
-                lhs = jnp.concatenate([f_buf[q, m, s] for s in range(entries)], axis=1)
-                rhs = jnp.concatenate([c_all[cols[q, s, m]] for s in range(entries)], axis=1)
-                done = lax.dot_general(lhs, rhs, NT, preferred_element_type=jnp.float32)
-                half[m, :, q * all_occ : (q + 1) * all_occ] = done.astype(jnp.bfloat16)
-            mine[m] = half[m, pl.ds(pl.multiple_of(occ * rows, rows), rows), :]
-            return carry
-
-        lax.fori_loop(n * step, (n + 1) * step, one, 0, unroll=2)
+    halves_of(0, nb, 1, True)
+
+    for k in range(1, NZ):
+        place_z(k, (z + NZ - k) % NZ).wait_recv()
+    fetch = pltpu.make_async_copy(by_z, place, p_in.at[0])
+    fetch.start()
 
     def pair(p, carry):
         lhs = mine[...].reshape(nb * rows, aux_count * all_occ)
@@ -160,12 +173,8 @@
         tiles[pl.ds((2 * p + 1) * nb, nb)] = prod[:, blk:].reshape(nb, rows, blk)
         return carry
 
-    lax.fori_loop(0, nb // 2, pair, 0, unroll=2)
-
-    for k in range(1, NZ):
-        place_z(k, (z + NZ - k) % NZ).wait_recv()
-    fetch = pltpu.make_async_copy(by_z, place, p_in.at[0])
-    fetch.start()
+    lax.fori_loop(0, nb // 2, pair, 0, unroll=6)
+
     fetch.wait()
 
     def post(n, part, axis_to):
@@ -254,12 +263,13 @@
 
     count = len(ORDER)
     for i in range(-AHEAD, count + LAG):
-        if i + AHEAD < count:
-            if ORDER[i + AHEAD] == 0:
-                merge_in()
+        if i + AHEAD < count - 1:
             first_hop(ORDER[i + AHEAD])
         if i == MERGE_AT:
             merge_out()
+        if i == count - 1 - LATE_BY:
+            merge_in()
+            first_hop(ORDER[-1])
         if 0 <= i < count:
             second_hop(ORDER[i])
         if i - LAG >= 0:
@@ -276,7 +286,7 @@
         for copy in copies(n, count, axis_to):
             copy.wait_send()
     for n in range(13):
-        pass_on(n, moves[n][0], moves[n][2], moves[n][3]).wait_send()
+        pass_on(n).wait_send()
     for k in range(1, NY):
         place_y(k, y).wait_send()
     for k in range(1, NZ):
@@ -301,7 +311,8 @@
             pltpu.SMEM((own,), jnp.int32),
             pltpu.VMEM(coeffs.shape[::-1], jnp.bfloat16),
             pltpu.VMEM(factor_tiles.shape, jnp.bfloat16),
-            pltpu.VMEM((nb, occ, blk), jnp.bfloat16),
+            pltpu.VMEM((nb, occ // 2, blk), jnp.bfloat16),
+            pltpu.VMEM((nb, occ // 2, blk), jnp.bfloat16),
             pltpu.VMEM((nb, blk, aux_count * occ), jnp.bfloat16),
             pltpu.VMEM((nb, rows, aux_count * occ), jnp.bfloat16),
             pltpu.VMEM((nb * nb, rows, blk), jnp.float32),

time: 69.2 us -> 65.2 us (0.942)
  Pallas kernels: 67.1 us -> 63.5 us
    pallas_call x1, Pallas kernels: 67.1 us -> 63.5 us  [shards(): pl.pallas_call(kernel, in_specs=[pl.BlockSpec(memory_space=pltpu.HBM)] *...]
where the time goes in v5:
time: 65.2 us; the launch traced here: 65 us
  Pallas kernels  63.5 us (97%)
  local copies, waits for them, and re-layouts  1.52 us (2%)
    pallas_call x1, Pallas kernels, shards(): pl.pallas_call(kernel, in_specs=[pl.BlockSpec(memory_space=pltpu.HBM)] *...  63.5 us
    unnamed x1, local copies, waits for them, and re-layouts  1.52 us

profile of v5, /device:TPU:1, one launch (start us, length us, event | category | flops | bytes accessed | tf_op | source)
XLA Modules:
  0.0 65.0 jit_solution(334577658412681806)
XLA Ops:
  0.0 63.5 %shard_map.46 = f32[9,16,128]{2,1,0:T(8,128)} custom-call(s32[2,4,24]{2,1,0:T(4,128)} %bitcast.3, s32[9]{0:T(128)} %owner_in.1, bf16[2,24,4,128,128]{4,3,2,1,0:T(8,128)(2,1)} %factor.1, bf16[32,3072]{1,0:T(8,128)(2,1)} %bitcast.2), custom_call_target="tpu_custom_call" | custom-call | tf_op jit(solution)/shard_map/pallas_call | solution.py:304
  63.5 1.5 %copy.6 = f32[9,16,128]{2,1,0:T(8,128)} copy(f32[9,16,128]{2,1,0:T(8,128)} %shard_map.46) | data formatting | bytes 147456

commit v6 on v5

--- a/solution.py
+++ b/solution.py
@@ -56,7 +56,8 @@
         load.start()
 
     barrier = pltpu.get_barrier_semaphore()
-    aux_peers = [up_y(k) for k in range(1, NY)] + [up_z(k) for k in range(1, NZ)]
+    reach = [1, 2, 3, 4, NZ - 1, NZ - 2, NZ - 3, NZ - 4]
+    aux_peers = [up_y(k) for k in range(1, NY)] + [up_z(k) for k in reach]
     occ_peers = [peer(1), peer(NX - 1), peer(0, True)]
     for other in aux_peers:
         pl.semaphore_signal(barrier, inc=1, device_id={"aux": other}, device_id_type=MESH)
@@ -116,8 +117,13 @@
     def place_y(k, row):
         return send(by_y.at[row], by_y.at[row], py_out.at[k - 1], py_in.at[k - 1], aux=up_y(k))
 
-    def place_z(k, row):
-        return send(by_z.at[row], by_z.at[row], pz_out.at[k - 1], pz_in.at[k - 1], aux=up_z(k))
+    rounds = [(k, 0) for k in reach]
+    rounds += [(4, NZ - k) for k in range(1, 5)] + [(NZ - 4, k) for k in range(1, 4)]
+
+    def place_z(n, receiving=False):
+        far, whose = rounds[n]
+        slot = (z + whose + (NZ - far if receiving else 0)) % NZ
+        return send(by_z.at[slot], by_z.at[slot], pz_out.at[n], pz_in.at[n], aux=up_z(far))
 
     for n in (0, 1, 2, 3, 6):
         go(n)
@@ -130,8 +136,8 @@
     for k in range(1, NY):
         place_y(k, (y + NY - k) % NY).wait_recv()
     by_z[z] = by_y[...]
-    for k in range(1, NZ):
-        place_z(k, z).start()
+    for n in range(len(reach)):
+        place_z(n).start()
     def halves_of(first, last, side, finish):
         def one(m, carry):
             for q in range(aux_count):
@@ -155,13 +161,17 @@
     for n, nxt in ((4, 11), (5, 12)):
         got(n)
         go(nxt)
+    for n in range(len(reach)):
+        place_z(n, True).wait_recv()
+    for n in range(len(reach), len(rounds)):
+        place_z(n).start()
     halves_of(nb // 4, nb, 0, False)
     for n in (8, 10, 11, 12):
         got(n)
     halves_of(0, nb, 1, True)
 
-    for k in range(1, NZ):
-        place_z(k, (z + NZ - k) % NZ).wait_recv()
+    for n in range(len(reach), len(rounds)):
+        place_z(n, True).wait_recv()
     fetch = pltpu.make_async_copy(by_z, place, p_in.at[0])
     fetch.start()
 
@@ -289,8 +299,8 @@
         pass_on(n).wait_send()
     for k in range(1, NY):
         place_y(k, y).wait_send()
-    for k in range(1, NZ):
-        place_z(k, z).wait_send()
+    for n in range(len(rounds)):
+        place_z(n).wait_send()
 
 
 def shards(factor_tiles, tile_cols, coeffs, pair_owner):

time: 65.2 us -> 62.8 us (0.963)
  the two profiles are of different devices: /device:TPU:1 before, /device:TPU:32 now
where the time goes in v6:
time: 62.8 us; the launch traced here: 62.7 us
  Pallas kernels  61.1 us (97%)
  local copies, waits for them, and re-layouts  1.52 us (2%)
    pallas_call x1, Pallas kernels, shards(): pl.pallas_call(kernel, in_specs=[pl.BlockSpec(memory_space=pltpu.HBM)] *...  61.1 us
    unnamed x1, local copies, waits for them, and re-layouts  1.52 us

profile of v6, /device:TPU:32, one launch (start us, length us, event | category | flops | bytes accessed | tf_op | source)
XLA Modules:
  0.0 62.7 jit_solution(1424334462163872705)
XLA Ops:
  0.0 61.1 %shard_map.46 = f32[9,16,128]{2,1,0:T(8,128)} custom-call(s32[2,4,24]{2,1,0:T(4,128)} %bitcast.3, s32[9]{0:T(128)} %owner_in.1, bf16[2,24,4,128,128]{4,3,2,1,0:T(8,128)(2,1)} %factor.1, bf16[32,3072]{1,0:T(8,128)(2,1)} %bitcast.2), custom_call_target="tpu_custom_call" | custom-call | tf_op jit(solution)/shard_map/pallas_call | solution.py:314
  61.1 1.5 %copy.6 = f32[9,16,128]{2,1,0:T(8,128)} copy(f32[9,16,128]{2,1,0:T(8,128)} %shard_map.46) | data formatting | bytes 147456

commit v7 on v6

--- a/solution.py
+++ b/solution.py
@@ -9,7 +9,7 @@
 NX, NY, NZ = 4, 4, 16
 MESH = pl.DeviceIdType.MESH
 ORDER = [8, 7, 9, 6, 10, 5, 11, 4, 12, 3, 13, 2, 14, 0]
-AHEAD, LAG, MID_AT, MERGE_AT, LATE_BY = 13, 7, 11, -9, 6
+AHEAD, LAG, MID_AT, MERGE_AT, LATE_BY = 13, 5, 10, -12, 5
 MESSAGES = 76
 STAGES = 4
 
@@ -83,7 +83,7 @@
         )
 
     def block(slot, part):
-        lo, count = (0, nb) if part is None else (part * (nb // 2), nb // 2)
+        lo, count = part[0] * (nb // 4), part[1] * (nb // 4)
         ref, at = (c_near, slot) if slot < 4 else (c_far, slot - 4)
         return ref.at[pl.ds(lo, count), pl.ds(at * share, share)]
 
@@ -93,19 +93,25 @@
 
     right, left, mate = peer(1), peer(NX - 1), peer(0, True)
     moves = [
-        (0, 2, 0, right),
-        (0, 4, 1, left),
-        (0, 2, 1, right),
-        (0, 4, 0, left),
-        (2, 6, 0, right),
-        (4, 6, 1, left),
-        (0, 1, None, mate),
-        (2, 3, 0, mate),
-        (4, 5, 1, mate),
-        (2, 3, 1, mate),
-        (4, 5, 0, mate),
-        (6, 7, 0, mate),
-        (6, 7, 1, mate),
+        (0, 2, (0, 1), right),
+        (0, 4, (2, 1), left),
+        (0, 2, (1, 1), right),
+        (0, 4, (3, 1), left),
+        (0, 2, (2, 2), right),
+        (0, 4, (0, 2), left),
+        (0, 1, (0, 4), mate),
+        (2, 6, (0, 1), right),
+        (4, 6, (2, 1), left),
+        (2, 6, (1, 1), right),
+        (4, 6, (3, 1), left),
+        (2, 3, (0, 2), mate),
+        (4, 5, (2, 2), mate),
+        (2, 3, (2, 2), mate),
+        (4, 5, (0, 2), mate),
+        (6, 7, (0, 1), mate),
+        (6, 7, (2, 1), mate),
+        (6, 7, (1, 1), mate),
+        (6, 7, (3, 1), mate),
     ]
 
     def go(n):
@@ -125,11 +131,11 @@
         slot = (z + whose + (NZ - far if receiving else 0)) % NZ
         return send(by_z.at[slot], by_z.at[slot], pz_out.at[n], pz_in.at[n], aux=up_z(far))
 
-    for n in (0, 1, 2, 3, 6):
+    for n in range(7):
         go(n)
     for k in range(1, NY):
         place_y(k, y).start()
-    for n, then in ((0, (4, 7)), (1, (5, 8)), (2, (9,)), (3, (10,))):
+    for n, then in ((0, (7,)), (1, (8,)), (2, (9, 11)), (3, (10, 12)), (4, (13,)), (5, (14,))):
         got(n)
         for nxt in then:
             go(nxt)
@@ -155,10 +161,10 @@
 
     for load in loads:
         load.wait()
-    for n in (6, 7, 9):
+    for n in (6, 11, 13):
         got(n)
     halves_of(0, nb // 4, 0, False)
-    for n, nxt in ((4, 11), (5, 12)):
+    for n, nxt in ((7, 15), (8, 16), (9, 17), (10, 18)):
         got(n)
         go(nxt)
     for n in range(len(reach)):
@@ -166,7 +172,7 @@
     for n in range(len(reach), len(rounds)):
         place_z(n).start()
     halves_of(nb // 4, nb, 0, False)
-    for n in (8, 10, 11, 12):
+    for n in (12, 14, 15, 16, 17, 18):
         got(n)
     halves_of(0, nb, 1, True)
 
@@ -295,7 +301,7 @@
     for n, count, axis_to in sent:
         for copy in copies(n, count, axis_to):
             copy.wait_send()
-    for n in range(13):
+    for n in range(len(moves)):
         pass_on(n).wait_send()
     for k in range(1, NY):
         place_y(k, y).wait_send()
@@ -337,7 +343,7 @@
             pltpu.VMEM((NY, own * rows, blk), jnp.float32),
             dma((3,)),
             dma((STAGES,)),
-            dma((13,)), dma((13,)),
+            dma((19,)), dma((19,)),
             dma((NY - 1,)), dma((NY - 1,)),
             dma((NZ - 1,)), dma((NZ - 1,)),
             dma((1,)),

time: 62.8 us -> 62.6 us (level)
  the two profiles are of different devices: /device:TPU:32 before, /device:TPU:2 now
where the time goes in v7:
time: 62.6 us; the launch traced here: 62.4 us
  Pallas kernels  60.9 us (97%)
  local copies, waits for them, and re-layouts  1.52 us (2%)
    pallas_call x1, Pallas kernels, shards(): pl.pallas_call(kernel, in_specs=[pl.BlockSpec(memory_space=pltpu.HBM)] *...  60.9 us
    unnamed x1, local copies, waits for them, and re-layouts  1.52 us

profile of v7, /device:TPU:2, one launch (start us, length us, event | category | flops | bytes accessed | tf_op | source)
XLA Modules:
  0.0 62.4 jit_solution(13646460325757039028)
XLA Ops:
  0.0 60.9 %shard_map.46 = f32[9,16,128]{2,1,0:T(8,128)} custom-call(s32[2,4,24]{2,1,0:T(4,128)} %bitcast.3, s32[9]{0:T(128)} %owner_in.1, bf16[2,24,4,128,128]{4,3,2,1,0:T(8,128)(2,1)} %factor.1, bf16[32,3072]{1,0:T(8,128)(2,1)} %bitcast.2), custom_call_target="tpu_custom_call" | custom-call | tf_op jit(solution)/shard_map/pallas_call | solution.py:320
  60.9 1.5 %copy.6 = f32[9,16,128]{2,1,0:T(8,128)} copy(f32[9,16,128]{2,1,0:T(8,128)} %shard_map.46) | data formatting | bytes 147456
